TPU v7x, 256 devices: a whole 4x4x8 slice. The times are simulated.
256 devices in a mesh: group: 16 (over z_hi, y, core), tensor: 16 (over x, z_lo).
Axes of the slice: x: 4, y: 4, z: 8 (z_hi: 2, z_lo: 4; z = z_hi * 4 + z_lo), core: 2. Of those that a mesh axis runs over, the one named last changes fastest.
Arguments:
- queries: bfloat16 [16384, 8192], P('group', 'tensor'), may hold values from -40 to 40
- resp_kv: bfloat16 [16384, 2048], P('group', 'tensor'), may hold values from -6 to 6
- prefix_kv: bfloat16 [4096, 2048], P('group', 'tensor'), may hold values from -6 to 6
- grad_out: bfloat16 [16384, 8192], P('group', 'tensor'), may hold values from -6 to 6
- lengths: int32 [128], P('group'), may hold values from 1 to 128, as said below
- slot_prompt: int32 [128], P('group'), may hold values from 0 to 7, as said below
Outputs:
- grad_queries: bfloat16 [16384, 8192], P('group', 'tensor')
- grad_resp_kv: bfloat16 [16384, 2048], P('group', 'tensor')
- grad_prefix_kv: bfloat16 [4096, 2048], P('group', 'tensor')
Inputs may be any that keep to these rules, and one draw needn't show every extreme that they name: `lengths`: each response's length; some response has length 128. `slot_prompt`: each of the 8 prompts is named by exactly 16 responses.
All inputs are finite; a program needn't handle non-finite values.
Results may differ from a plain program's by a relative error of at most 0.01.
Values may be sent and summed in bfloat16 or wider, within the bound.
A program may use at most 64 MiB of HBM per device.

v0:
```python
import jax
import jax.numpy as jnp
from jax import lax
from jax.sharding import PartitionSpec as P

HD = 128
RL = 128
PL = 512


def partner(array, axis, stride):
    return lax.ppermute(array, axis, [(i, i ^ 1 << stride) for i in range(lax.axis_size(axis))])


def shards(queries, resp_kv, prefix_kv, grad_out, lengths, slot_prompt):
    scale = HD ** (-0.5)
    even = lax.axis_index("tensor") % 2 == 0
    other_resp, other_local = partner((resp_kv, prefix_kv), "tensor", 0)
    own_all, other_all = (
        lax.all_gather(prefix_kv, "group", axis=0, tiled=True),
        lax.all_gather(other_local, "group", axis=0, tiled=True),
    )
    resp_keys = jnp.where(even, resp_kv, other_resp)
    resp_vals = jnp.where(even, other_resp, resp_kv)
    pref_keys = jnp.where(even, own_all, other_all)
    pref_vals = jnp.where(even, other_all, own_all)
    slots = lengths.shape[0]
    heads = queries.shape[1] // HD
    prompts = pref_keys.shape[0] // PL
    pref_keys = pref_keys.reshape(prompts, PL, HD)
    pref_vals = pref_vals.reshape(prompts, PL, HD)
    qs = queries.reshape(slots, RL, heads, HD)
    gos = grad_out.reshape(slots, RL, heads, HD)
    rks = resp_keys.reshape(slots, RL, HD)
    rvs = resp_vals.reshape(slots, RL, HD)
    pos = jnp.arange(RL, dtype=jnp.int32)
    allowed = jnp.concatenate(
        [jnp.ones((RL, PL), dtype=bool), pos[None, :] <= pos[:, None]], axis=1
    )
    dq_list = []
    rk_grads = []
    rv_grads = []
    pk_grads = []
    pv_grads = []
    for slot in range(slots):
        q_s = qs[slot]
        go_s = gos[slot]
        index = slot_prompt[slot]
        keys = jnp.concatenate(
            [lax.dynamic_index_in_dim(pref_keys, index, 0, keepdims=False), rks[slot]], axis=0
        )
        vals = jnp.concatenate(
            [lax.dynamic_index_in_dim(pref_vals, index, 0, keepdims=False), rvs[slot]], axis=0
        )
        scores = jnp.einsum("igd,jd->gij", q_s, keys, preferred_element_type=jnp.float32) * scale
        scores = jnp.where(allowed[None], scores, -1e30)
        top = jnp.max(scores, axis=-1, keepdims=True)
        expo = jnp.exp(scores - top)
        probs = expo / jnp.sum(expo, axis=-1, keepdims=True)
        probs_b = probs.astype(jnp.bfloat16)
        attended = jnp.einsum("gij,jd->igd", probs_b, vals, preferred_element_type=jnp.float32)
        live = pos < lengths[slot]
        dout = jnp.where(live[:, None, None], go_s, jnp.zeros_like(go_s))
        delta = jnp.sum(dout.astype(jnp.float32) * attended, axis=-1)
        dprob = jnp.einsum("igd,jd->gij", dout, vals, preferred_element_type=jnp.float32)
        dscore = (probs * (dprob - jnp.transpose(delta)[:, :, None]) * scale).astype(jnp.bfloat16)
        dq_list.append(
            jnp.einsum("gij,jd->igd", dscore, keys, preferred_element_type=jnp.float32).astype(
                jnp.bfloat16
            )
        )
        dk = jnp.einsum("gij,igd->jd", dscore, q_s, preferred_element_type=jnp.float32)
        dv = jnp.einsum("gij,igd->jd", probs_b, dout, preferred_element_type=jnp.float32)
        pk_grads.append(dk[:PL])
        pv_grads.append(dv[:PL])
        rk_grads.append(dk[PL:])
        rv_grads.append(dv[PL:])
    grad_queries = jnp.stack(dq_list, axis=0).reshape(slots * RL, heads * HD)
    resp_dk = jnp.concatenate(rk_grads, axis=0)
    resp_dv = jnp.concatenate(rv_grads, axis=0)
    resp_keep = jnp.where(even, resp_dk, resp_dv)
    resp_send = jnp.where(even, resp_dv, resp_dk)
    resp_recv = partner(resp_send, "tensor", 0)
    grad_resp_kv = (resp_keep + resp_recv).astype(jnp.bfloat16)
    owners = (slot_prompt[None, :] == jnp.arange(prompts, dtype=jnp.int32)[:, None]).astype(
        jnp.float32
    )
    accum_k = jnp.einsum(
        "ps,sjd->pjd", owners, jnp.stack(pk_grads, axis=0), precision=lax.Precision.HIGHEST
    )
    accum_v = jnp.einsum(
        "ps,sjd->pjd", owners, jnp.stack(pv_grads, axis=0), precision=lax.Precision.HIGHEST
    )
    total_rows = prompts * PL
    wide = jnp.concatenate([accum_k, accum_v], axis=-1).reshape(total_rows, 2 * HD)
    summed = lax.psum_scatter(wide, "group", scatter_dimension=0, tiled=True)
    keep_part = jnp.where(even, summed[:, :HD], summed[:, HD:])
    send_part = jnp.where(even, summed[:, HD:], summed[:, :HD])
    recv_part = partner(send_part.astype(jnp.bfloat16), "tensor", 0).astype(send_part.dtype)
    grad_prefix_kv = (keep_part + recv_part).astype(jnp.bfloat16)
    return (grad_queries, grad_resp_kv, grad_prefix_kv)


def solution(mesh):
    return jax.shard_map(
        shards,
        mesh=mesh,
        in_specs=(
            P("group", "tensor"),
            P("group", "tensor"),
            P("group", "tensor"),
            P("group", "tensor"),
            P("group"),
            P("group"),
        ),
        out_specs=(P("group", "tensor"), P("group", "tensor"), P("group", "tensor")),
        check_vma=False,
    )
```

profile of v0, /device:TPU:6, one launch (start us, length us, event | category | flops | bytes accessed | tf_op | source)
XLA Modules:
  0.0 300.4 jit_solution(14138830810213378901)
XLA Ops:
  8.0 2.0 collective-permute-start
  10.1 1.6 fusion.245
  18.3 1.6 fusion.246
  49.7 19.7 %all-gather.3.cloned.1.call-done = bf16[4096,128]{1,0:T(8,128)(2,1)} async-done(((bf16[256,128]{1,0:T(8,128)(2,1)}), bf16[4096,128]{1,0:T(8,128)(2,1)}) %all-gather.3.cloned.1.call-update) | async-done | bytes 1048592 | tf_op jit(solution)/shard_map/all_gather | solution.py:20
  69.4 54.7 %all-gather.5.cloned.1.call-done = bf16[4096,128]{1,0:T(8,128)(2,1)} async-done(((bf16[256,128]{1,0:T(8,128)(2,1)}), bf16[4096,128]{1,0:T(8,128)(2,1)}) %all-gather.5.cloned.1.call-update) | async-done | bytes 1048592 | tf_op jit(solution)/shard_map/all_gather | solution.py:21
  124.1 1.7 broadcast_select_fusion
  134.9 1.6 fusion.249
  140.8 1.6 fusion.250
  144.9 1.7 fusion.71
  147.7 1.6 fusion.251
  149.4 1.5 fusion.112
  154.3 2.7 fusion.252
  157.0 1.5 fusion.113
  162.1 2.6 fusion.253
  164.7 1.6 fusion.114
  170.1 2.6 fusion.254
  172.7 1.5 fusion.115
  178.3 2.2 fusion.8
  181.9 2.2 fusion.10
  184.4 3.2 %copy.150 = f32[8,512,256]{2,1,0:T(8,128)} copy(f32[8,512,256]{2,0,1:T(8,128)S(1)} %pad_maximum_fusion) | data formatting | bytes 8388608 | tf_op jit(solution)/shard_map/concatenate | solution.py:95
  211.2 1.7 copy.232
  214.1 73.8 %reduce-scatter.2.cloned.1.call-done = f32[256,256]{1,0:T(8,128)} async-done(((f32[4096,256]{1,0:T(8,128)}), f32[256,256]{1,0:T(8,128)}) %reduce-scatter.2.cloned.1.call-update) | async-done | bytes 262160 | tf_op jit(solution)/shard_map/reduce_scatter | solution.py:96
  289.6 1.8 add_convert_fusion
  291.4 1.8 collective-permute-done.3
  (311 shorter events, 82.0 us)
Async XLA Ops:
  7.2 14.1 %copy-start.31 = (bf16[1024,512]{1,0:T(8,128)(2,1)S(1)}, bf16[1024,512]{1,0:T(8,128)(2,1)}, u32[]{:S(2)}) copy-start(bf16[1024,512]{1,0:T(8,128)(2,1)} %param.9) | copy-start | bytes 3145732
  7.2 62.3 %all-gather.3.cloned.1.call-start = ((), (), s32[]{:S(2)}) async-start(), calls=%async_computation.1 | async-start | bytes 1114112 | tf_op jit(solution)/shard_map/all_gather | solution.py:20
  7.9 116.2 %all-gather.5.cloned.1.call-start = ((), (), s32[]{:S(2)}) async-start(), calls=%async_computation.2 | async-start | bytes 1114112 | tf_op jit(solution)/shard_map/all_gather | solution.py:21
  8.0 5.0 %collective-permute-start = (bf16[256,128]{1,0:T(8,128)(2,1)}, bf16[256,128]{1,0:T(8,128)(2,1)S(1)}, u32[]{:S(2)}, u32[]{:S(2)}) collective-permute-start(bf16[256,128]{1,0:T(8,128)(2,1)} %param.8), channel_id=1, source_target_pairs={{0,1},{1,0},{2,3},{3,2},{4,5},{5,4},{6,7},{7,6},{8,9},{9,8},{10,11... | collective-permute-start | bytes 196616 | tf_op jit(solution)/shard_map/ppermute | solution.py:12
  10.0 37.9 %collective-permute-start.1 = (bf16[1024,128]{1,0:T(8,128)(2,1)}, bf16[1024,128]{1,0:T(8,128)(2,1)}, u32[]{:S(2)}, u32[]{:S(2)}) collective-permute-start(bf16[1024,128]{1,0:T(8,128)(2,1)} %param.7), channel_id=1, source_target_pairs={{0,1},{1,0},{2,3},{3,2},{4,5},{5,4},{6,7},{7,6},{8,9},{9,8},{10,11... | collective-permute-start | bytes 786440 | tf_op jit(solution)/shard_map/ppermute | solution.py:12
  13.6 274.3 %reduce-scatter.2.cloned.1.call-start = ((), (), s32[]{:S(2)}) async-start(), calls=%async_computation.3 | async-start | bytes 4456448 | tf_op jit(solution)/shard_map/reduce_scatter | solution.py:96
  36.0 11.9 %copy-start.56 = (bf16[1024,128]{1,0:T(8,128)(2,1)S(1)}, bf16[1024,128]{1,0:T(8,128)(2,1)}, u32[]{:S(2)}) copy-start(bf16[1024,128]{1,0:T(8,128)(2,1)} %param.7) | copy-start | bytes 786436
  46.6 80.4 %copy-start.75 = (pred[128,640]{0,1:T(8,128)(4,1)}, pred[128,640]{0,1:T(8,128)(4,1)S(1)}, u32[]{:S(2)}) copy-start(pred[128,640]{0,1:T(8,128)(4,1)S(1)} %concatenate.61) | copy-start | bytes 245764
  49.7 77.3 %copy-start.73 = (bf16[128,128]{1,0:T(8,128)(2,1)}, bf16[128,128]{1,0:T(8,128)(2,1)S(1)}, u32[]{:S(2)}) copy-start(bf16[128,128]{1,0:T(8,128)(2,1)S(1)} %get-tuple-element.90) | copy-start | bytes 98308
  127.0 3.6 %copy-start.45 = (bf16[512,128]{1,0:T(8,128)(2,1)}, bf16[512,128]{1,0:T(8,128)(2,1)S(1)}, u32[]{:S(2)}) copy-start(bf16[512,128]{1,0:T(8,128)(2,1)S(1)} %get-tuple-element.99) | copy-start | bytes 393220
  174.6 3.7 %copy-start.29 = (f32[640,128]{1,0:T(8,128)}, f32[640,128]{1,0:T(8,128)S(1)}, u32[]{:S(2)}) copy-start(f32[640,128]{1,0:T(8,128)S(1)} %convolution_bitcast_fusion.8) | copy-start | bytes 983044
  176.5 5.3 %copy-start.30 = (f32[640,128]{1,0:T(8,128)}, f32[640,128]{1,0:T(8,128)S(1)}, u32[]{:S(2)}) copy-start(f32[640,128]{1,0:T(8,128)S(1)} %convolution_bitcast_fusion.16) | copy-start | bytes 983044
  194.4 9.0 %copy-start.48 = (bf16[512,128]{1,0:T(8,128)(2,1)S(1)}, bf16[512,128]{1,0:T(8,128)(2,1)}, u32[]{:S(2)}) copy-start(bf16[512,128]{1,0:T(8,128)(2,1)} %copy-done.47) | copy-start | bytes 393220
  194.4 9.0 %copy-start.74 = (bf16[128,128]{1,0:T(8,128)(2,1)S(1)}, bf16[128,128]{1,0:T(8,128)(2,1)}, u32[]{:S(2)}) copy-start(bf16[128,128]{1,0:T(8,128)(2,1)} %copy-done.73) | copy-start | bytes 98308
  200.4 4.0 %copy-start.8 = (f32[1024,128]{1,0:T(8,128)}, f32[1024,128]{1,0:T(8,128)S(1)}, u32[]{:S(2)}) copy-start(f32[1024,128]{1,0:T(8,128)S(1)} %constant_dynamic-update-slice_fusion.8) | copy-start | bytes 1572868
  200.4 4.0 %copy-start.46 = (bf16[512,128]{1,0:T(8,128)(2,1)S(1)}, bf16[512,128]{1,0:T(8,128)(2,1)}, u32[]{:S(2)}) copy-start(bf16[512,128]{1,0:T(8,128)(2,1)} %copy-done.45) | copy-start | bytes 393220
  200.4 4.0 %copy-start.72 = (bf16[128,128]{1,0:T(8,128)(2,1)S(1)}, bf16[128,128]{1,0:T(8,128)(2,1)}, u32[]{:S(2)}) copy-start(bf16[128,128]{1,0:T(8,128)(2,1)} %get-tuple-element.91) | copy-start | bytes 98308
  202.5 3.9 %copy-start.43 = (bf16[512,128]{1,0:T(8,128)(2,1)S(1)}, bf16[512,128]{1,0:T(8,128)(2,1)}, u32[]{:S(2)}) copy-start(bf16[512,128]{1,0:T(8,128)(2,1)} %get-tuple-element.101) | copy-start | bytes 393220
  202.5 3.9 %copy-start.69 = (bf16[128,128]{1,0:T(8,128)(2,1)S(1)}, bf16[128,128]{1,0:T(8,128)(2,1)}, u32[]{:S(2)}) copy-start(bf16[128,128]{1,0:T(8,128)(2,1)} %get-tuple-element.93) | copy-start | bytes 98308
  202.5 87.1 %collective-permute-start.2 = (f32[1024,128]{1,0:T(8,128)}, f32[1024,128]{1,0:T(8,128)}, u32[]{:S(2)}, u32[]{:S(2)}) collective-permute-start(f32[1024,128]{1,0:T(8,128)} %broadcast_select_fusion.2), channel_id=1, source_target_pairs={{0,1},{1,0},{2,3},{3,2},{4,5},{5,4},{6,7},{7,6},{8,9},{9,8},{10,11... | collective-permute-start | bytes 1572872 | tf_op jit(solution)/shard_map/ppermute | solution.py:12
  212.9 76.7 %copy-start.7 = (f32[1024,128]{1,0:T(8,128)S(1)}, f32[1024,128]{1,0:T(8,128)}, u32[]{:S(2)}) copy-start(f32[1024,128]{1,0:T(8,128)} %copy-done.6) | copy-start | bytes 1572868
  212.9 76.7 %copy-start.9 = (f32[1024,128]{1,0:T(8,128)S(1)}, f32[1024,128]{1,0:T(8,128)}, u32[]{:S(2)}) copy-start(f32[1024,128]{1,0:T(8,128)} %copy-done.8) | copy-start | bytes 1572868
  287.8 5.4 %copy-start.32 = (f32[256,256]{1,0:T(8,128)S(1)}, f32[256,256]{1,0:T(8,128)}, u32[]{:S(2)}) copy-start(f32[256,256]{1,0:T(8,128)} %reduce-scatter.2.cloned.1.call-done) | copy-start | bytes 786436
  288.9 4.4 %collective-permute-start.3 = (bf16[256,128]{1,0:T(8,128)(2,1)S(1)}, bf16[256,128]{1,0:T(8,128)(2,1)S(1)}, u32[]{:S(2)}, u32[]{:S(2)}) collective-permute-start(bf16[256,128]{1,0:T(8,128)(2,1)S(1)} %select_convert_fusion), channel_id=1, source_target_pairs={{0,1},{1,0},{2,3},{3,2},{4,5},{5,4},{6,7},{7,6},{8,9},{9,8},{10,11... | collective-permute-start | bytes 196616 | tf_op jit(solution)/shard_map/ppermute | solution.py:12
  (76 other events, 141.2 us)
Sparse Core Ops, SparseCore 0:
  10.7 58.6 all-gather.2
  72.7 51.3 all-gather.4
  187.8 100.0 reduce-scatter.1
where the time goes:
time: 302 us; the launch traced here: 300 us
  waiting for transfers between devices  151 us (50%)
  matrix products  48.2 us (16%)
  local copies, waits for them, and re-layouts  45.5 us (15%)
  between operations  29.9 us (10%)
  other arithmetic  22.2 us (7%)
  starting transfers between devices  3.91 us (1%)
    reduce_scatter x1, waiting for transfers between devices, shards(): summed = lax.psum_scatter(wide, 'group', scatter_dimension=0, tiled=True)  73.8 us
    all_gather x1, waiting for transfers between devices, shards(): lax.all_gather(other_local, 'group', axis=0, tiled=True)  54.7 us
    unnamed x224, local copies, waits for them, and re-layouts  28.2 us
    all_gather x1, waiting for transfers between devices, shards(): lax.all_gather(prefix_kv, 'group', axis=0, tiled=True)  19.7 us
    sub x8, matrix products, shards(): expo = jnp.exp(scores - top)  13.8 us
    lt x8, other arithmetic, shards(): live = pos < lengths[slot]  8.26 us
    dot_general x8, matrix products, shards(): jnp.einsum('gij,igd->jd', probs_b, dout, preferred_element_type=jnp.float32)  7.88 us
    dot_general x8, matrix products, shards(): jnp.einsum('gij,igd->jd', dscore, q_s, preferred_element_type=jnp.float32)  7.84 us
  transfers between devices with their start and end apart: 7, of which 4 were waited for; matrix products, arithmetic and copies ran while one was open for 17% of the time, Pallas kernels for 0%

commit v1 on v0

v1 whole, which is shorter than its diff:
```python
import functools

import jax
import jax.numpy as jnp
from jax import lax
from jax.experimental import pallas as pl
from jax.experimental.pallas import tpu as pltpu
from jax.sharding import PartitionSpec as P

HD = 128
RL = 128
PL = 512
NP = 8
NS = 8
NH = 4
HALF = PL // 2
COLS = NH * RL
SCALE = HD ** (-0.5)
EXP2 = SCALE * 1.4426950408889634
F32 = jnp.float32
BF16 = jnp.bfloat16
MESH = pl.DeviceIdType.MESH
SENDS = 64


def nt(a, b):
    return lax.dot_general(a, b, (((1,), (1,)), ((), ())), preferred_element_type=F32)


def nn(a, b):
    return lax.dot_general(a, b, (((1,), (0,)), ((), ())), preferred_element_type=F32)


def tn(a, b):
    return lax.dot_general(a, b, (((0,), (0,)), ((), ())), preferred_element_type=F32)


def forward_part(q, do, keys, vals, causal):
    scores = nt(keys, q)
    if causal:
        row = lax.broadcasted_iota(jnp.int32, scores.shape, 0)
        col = lax.broadcasted_iota(jnp.int32, scores.shape, 1) % RL
        scores = jnp.where(row <= col, scores, -1e30)
    top = jnp.max(scores, axis=0, keepdims=True)
    expo = jnp.exp2((scores - top) * EXP2)
    dprob = nt(vals, do)
    total = jnp.sum(expo, axis=0, keepdims=True)
    delta = jnp.sum(expo * dprob, axis=0, keepdims=True)
    return expo, dprob, top, total, delta


def kernel(sp_ref, len_ref, q_hbm, do_hbm, resp_hbm, pref_hbm,
           dq_hbm, dr_ref, dp_out,
           own, sib, resp, q_v, do_v, e_ref, dp_ref, ds_ref, st_ref, run,
           rg, rg_send, rg_recv, sib_send, sib_recv, g_ref, y_recv, z_send, z_recv, dq_v, prev_ref, last_ref,
           load_sem, out_sem, send_sem, own_sem, sib_sem, back_sem, y_sem, z_sem, resp_sem, rg_sem):
    group, tensor = lax.axis_index("group"), lax.axis_index("tensor")
    zh, y, c, kv = group // 8, (group // 2) % 4, group % 2, tensor % 2
    pair = tensor + 1 - 2 * kv

    def device(dz, dy, dc, dl):
        g = ((zh + dz) % 2) * 8 + ((y + dy) % 4) * 2 + (c + dc) % 2
        return (g, pair if dl else tensor)

    peers = [(0, 0, 1, 0), (0, 0, 0, 1), (1, 0, 0, 0), (1, 0, 0, 1), (0, 1, 0, 0), (0, 2, 0, 0), (0, 3, 0, 0)]
    flying = []

    def send(src, dst, recv_sem, to):
        copy = pltpu.make_async_remote_copy(
            src, dst, send_sem.at[len(flying)], recv_sem, device_id=device(*to), device_id_type=MESH
        )
        copy.start()
        flying.append(copy)

    def arrived(ref, recv_sem):
        pltpu.make_async_remote_copy(
            ref, ref, send_sem.at[0], recv_sem, device_id=device(0, 0, 1, 0), device_id_type=MESH
        ).wait_recv()

    mine = zh * 4 + y
    loads = [
        pltpu.make_async_copy(pref_hbm, own.at[kv, mine], load_sem.at[8]),
        pltpu.make_async_copy(resp_hbm, resp.at[kv], load_sem.at[9]),
    ]
    for i, (src, dst) in enumerate(((q_hbm, q_v), (do_hbm, do_v))):
        for h in range(NH):
            loads.append(
                pltpu.make_async_copy(
                    src.at[:, :, pl.ds(h * HD, HD)], dst.at[:, pl.ds(h * RL, RL), :], load_sem.at[i * NH + h]
                )
            )
    for copy in loads:
        copy.start()
    barrier = pltpu.get_barrier_semaphore()
    for to in peers:
        pl.semaphore_signal(barrier, inc=1, device_id=device(*to), device_id_type=MESH)
    pl.semaphore_wait(barrier, len(peers))

    def unit(dz, dy, dl):
        return ((kv + dl) % 2, ((zh + dz) % 2) * 4 + (y + dy) % 4)

    def spread(k, p, targets):
        for to in targets:
            send(own.at[k, p], own.at[k, p], own_sem.at[k, p], to)
        send(own.at[k, p], sib.at[k, p], sib_sem.at[k, p], (0, 0, 1, 0))

    loads[0].wait()
    spread(kv, mine, peers[1:])
    for dz, dl in ((0, 1), (1, 1), (1, 0)):
        k, p = unit(dz, 0, dl)
        arrived(own.at[k, p], own_sem.at[k, p])
        spread(k, p, peers[4:])
    loads[1].wait()
    send(resp.at[kv], resp.at[kv], resp_sem.at[0], (0, 0, 0, 1))

    for s in range(NS):
        at = jnp.int32(-1)
        for j in range(s):
            at = jnp.where(sp_ref[j] == sp_ref[s], j, at)
        prev_ref[s] = at
    for p in range(NP):
        at = jnp.int32(-1)
        for j in range(NS):
            at = jnp.where(sp_ref[j] == p, j, at)
        last_ref[p] = at
    for copy in loads[2:]:
        copy.wait()

    @pl.loop(0, NS)
    def _(s):
        row = lax.broadcasted_iota(jnp.int32, (COLS, HD), 0) % RL
        do_v[s] = jnp.where(row < len_ref[s], do_v[s], jnp.zeros((COLS, HD), BF16))

    for dz, dl in ((0, 0), (0, 1), (1, 1), (1, 0)):
        for dy in (1, 3, 2):
            k, p = unit(dz, dy, dl)
            arrived(own.at[k, p], own_sem.at[k, p])
            spread(k, p, ())

    def forward(keys, vals, part):
        n = RL if part == 2 else HALF

        @pl.loop(0, NS)
        def _(s):
            at = s if part == 2 else sp_ref[s]
            expo, dprob, top, total, delta = forward_part(q_v[s], do_v[s], keys[at], vals[at], part == 2)
            e_ref[s, pl.ds(part * HALF, n)] = expo
            dp_ref[s, pl.ds(part * HALF, n)] = dprob
            st_ref[s, pl.ds(part, 1)] = top
            st_ref[s, pl.ds(3 + part, 1)] = total
            st_ref[s, pl.ds(6 + part, 1)] = delta

    forward(own.at[0], own.at[1], 0)
    arrived(resp.at[1 - kv], resp_sem.at[0])
    forward(resp.at[0], resp.at[1], 2)
    for k in range(2):
        for p in range(NP):
            arrived(sib.at[k, p], sib_sem.at[k, p])
    forward(sib.at[0], sib.at[1], 1)

    @pl.loop(0, NS)
    def _(s):
        tops = st_ref[s, pl.ds(0, 3)]
        factor = jnp.exp2((tops - jnp.max(tops, axis=0, keepdims=True)) * EXP2)
        factor = factor / jnp.sum(factor * st_ref[s, pl.ds(3, 3)], axis=0, keepdims=True)
        st_ref[s, pl.ds(0, 3)] = factor
        st_ref[s, pl.ds(3, 1)] = jnp.sum(factor * st_ref[s, pl.ds(6, 3)], axis=0, keepdims=True)

    def backward(s, part):
        rows = pl.ds(part * HALF, RL if part == 2 else HALF)
        prob = e_ref[s, rows] * st_ref[s, pl.ds(part, 1)]
        ds = (prob * (dp_ref[s, rows] - st_ref[s, pl.ds(3, 1)])).astype(BF16)
        ds_ref[s, rows] = ds
        return nn(ds, q_v[s]) * SCALE, nn(prob.astype(BF16), do_v[s])

    @pl.loop(0, NS)
    def _(s):
        for k, grad in enumerate(backward(s, 2)):
            rg[k, s] = grad
            rg_send[k, s] = grad.astype(BF16)

    send(rg_send.at[1 - kv], rg_recv, rg_sem.at[0], (0, 0, 0, 1))

    def prefix_grads(part):
        @pl.loop(0, NS)
        def _(s):
            prev = prev_ref[s]
            at = jnp.maximum(prev, 0)
            for k, grad in enumerate(backward(s, part)):
                run[k, s] = grad + jnp.where(prev >= 0, run[k, at], 0.0)

    def total_of(k, p):
        last = last_ref[p]
        return jnp.where(last >= 0, run[k, jnp.maximum(last, 0)], 0.0)

    prefix_grads(1)
    for k in range(2):
        @pl.loop(0, NP)
        def _(p, k=k):
            sib_send[k, p] = total_of(k, p).astype(BF16)
        send(sib_send.at[k], sib_recv.at[k], back_sem.at[k], (0, 0, 1, 0))
    prefix_grads(0)
    for k in range(2):
        arrived(sib_recv.at[k], back_sem.at[k])

        @pl.loop(0, NP)
        def _(p, k=k):
            g_ref[k, p // 4, p % 4] = (total_of(k, p) + sib_recv[k, p].astype(F32)).astype(BF16)
        for dy in (1, 3, 2):
            send(g_ref.at[k, :, (y + dy) % 4], y_recv.at[dy - 1, k], y_sem.at[dy - 1, k], (0, dy, 0, 0))

    @pl.loop(0, NS)
    def _(s):
        p = sp_ref[s]
        dqt = (
            tn(own[0, p], ds_ref[s, pl.ds(0, HALF)])
            + tn(sib[0, p], ds_ref[s, pl.ds(HALF, HALF)])
            + tn(resp[0, s], ds_ref[s, pl.ds(PL, RL)])
        ) * SCALE
        for h in range(NH):
            dq_v[s, :, pl.ds(h * HD, HD)] = dqt[:, h * RL:(h + 1) * RL].T.astype(BF16)

    dq_out = pltpu.make_async_copy(dq_v, dq_hbm, out_sem.at[0])
    dq_out.start()
    arrived(rg_recv, rg_sem.at[0])

    @pl.loop(0, NS)
    def _(s):
        dr_ref[s] = (rg[kv, s] + rg_recv[s].astype(F32)).astype(BF16)

    def chip_total(k, z):
        total = g_ref[k, z, y].astype(F32)
        for i in range(3):
            total = total + y_recv[i, k, z].astype(F32)
        return total

    for k in range(2):
        for dy in (1, 3, 2):
            arrived(y_recv.at[dy - 1, k], y_sem.at[dy - 1, k])
    for i, (dz, dl) in enumerate(((1, 0), (1, 1), (0, 1))):
        k, z = (kv + dl) % 2, (zh + dz) % 2
        z_send[i] = chip_total(k, z).astype(BF16)
        send(z_send.at[i], z_recv.at[i], z_sem.at[i], (dz, 0, 0, dl))
    total = chip_total(kv, zh)
    for i in (2, 1, 0):
        arrived(z_recv.at[i], z_sem.at[i])
        total = total + z_recv[i].astype(F32)
    dp_out[...] = total.astype(BF16)
    dq_out.wait()
    for copy in flying:
        copy.wait_send()


def shards(queries, resp_kv, prefix_kv, grad_out, lengths, slot_prompt):
    smem = pl.BlockSpec(memory_space=pltpu.SMEM)
    vmem = pl.BlockSpec(memory_space=pltpu.VMEM)
    hbm = pl.BlockSpec(memory_space=pl.ANY)
    dma = pltpu.SemaphoreType.DMA
    dq, dr, dp = pl.pallas_call(
        kernel,
        out_shape=[
            jax.ShapeDtypeStruct((NS, RL, COLS), BF16),
            jax.ShapeDtypeStruct((NS, RL, HD), BF16),
            jax.ShapeDtypeStruct((HALF, HD), BF16),
        ],
        in_specs=[smem, smem, hbm, hbm, hbm, hbm],
        out_specs=[hbm, vmem, vmem],
        scratch_shapes=[
            pltpu.VMEM((2, NP, HALF, HD), BF16),
            pltpu.VMEM((2, NP, HALF, HD), BF16),
            pltpu.VMEM((2, NS, RL, HD), BF16),
            pltpu.VMEM((NS, COLS, HD), BF16),
            pltpu.VMEM((NS, COLS, HD), BF16),
            pltpu.VMEM((NS, PL + RL, COLS), F32),
            pltpu.VMEM((NS, PL + RL, COLS), F32),
            pltpu.VMEM((NS, PL + RL, COLS), BF16),
            pltpu.VMEM((NS, 16, COLS), F32),
            pltpu.VMEM((2, NS, HALF, HD), F32),
            pltpu.VMEM((2, NS, RL, HD), F32),
            pltpu.VMEM((2, NS, RL, HD), BF16),
            pltpu.VMEM((NS, RL, HD), BF16),
            pltpu.VMEM((2, NP, HALF, HD), BF16),
            pltpu.VMEM((2, NP, HALF, HD), BF16),
            pltpu.VMEM((2, 2, 4, HALF, HD), BF16),
            pltpu.VMEM((3, 2, 2, HALF, HD), BF16),
            pltpu.VMEM((3, HALF, HD), BF16),
            pltpu.VMEM((3, HALF, HD), BF16),
            pltpu.VMEM((NS, RL, COLS), BF16),
            pltpu.SMEM((NS,), jnp.int32),
            pltpu.SMEM((NP,), jnp.int32),
            dma((10,)),
            dma((1,)),
            dma((SENDS,)),
            dma((2, NP)),
            dma((2, NP)),
            dma((2,)),
            dma((3, 2)),
            dma((3,)),
            dma((1,)),
            dma((1,)),
        ],
        compiler_params=pltpu.CompilerParams(
            collective_id=0, has_side_effects=True, vmem_limit_bytes=56 * 2**20
        ),
    )(
        slot_prompt,
        lengths,
        queries.reshape(NS, RL, COLS),
        grad_out.reshape(NS, RL, COLS),
        resp_kv.reshape(NS, RL, HD),
        prefix_kv,
    )
    return dq.reshape(NS * RL, COLS), dr.reshape(NS * RL, HD), dp


def solution(mesh):
    spec = P("group", "tensor")
    return jax.shard_map(
        shards,
        mesh=mesh,
        in_specs=(spec, spec, spec, spec, P("group"), P("group")),
        out_specs=(spec, spec, spec),
        check_vma=False,
    )
```

time: 302 us -> 66.2 us (0.22)
  waiting for transfers between devices: 151 us -> 0 us
  Pallas kernels: 0 us -> 61.5 us
  matrix products: 48.2 us -> 0 us
  local copies, waits for them, and re-layouts: 45.5 us -> 3.8 us
  between operations: 29.9 us -> 0.65 us
  other arithmetic: 22.2 us -> 0 us
  starting transfers between devices: 3.91 us -> 0 us
    all_gather x2 -> x0, waiting for transfers between devices: 74.4 us -> none  [the longest x1 54.7 us: shards(): lax.all_gather(other_local, 'group', axis=0, tiled=True)]
    reduce_scatter x1 -> x0, waiting for transfers between devices: 73.8 us -> none  [shards(): summed = lax.psum_scatter(wide, 'group', scatter_dimension=0, tiled=True)]
    pallas_call x0 -> x1, Pallas kernels: none -> 61.5 us  [shards(): pl.pallas_call(kernel, out_shape=[jax.ShapeDtypeStruct((NS, RL, COLS), BF...]
    dot_general x42 -> x0, matrix products: 34.4 us -> none  [the longest x8 7.88 us: shards(): jnp.einsum('gij,igd->jd', probs_b, dout, preferred_element_type=jnp.float32)]
    unnamed x224 -> x7, local copies, waits for them, and re-layouts: 28.2 us -> 3.8 us
    sub x8 -> x0, matrix products: 13.8 us -> none  [shards(): expo = jnp.exp(scores - top)]
    slice x13 -> x0, local copies, waits for them, and re-layouts: 10.9 us -> none  [the longest x9 5.47 us: shards(): go_s = gos[slot]]
    convert_element_type x11 -> x0, other arithmetic: 9.99 us -> none  [the longest x8 6.49 us: shards(): probs_b = probs.astype(jnp.bfloat16)]
  transfers between devices with their start and end apart: 7 -> 0, of which waited for: 4 -> 0; matrix products, arithmetic and copies ran while one was open for 17% -> 0% of each run, Pallas kernels for 0% -> 0%
where the time goes in v1:
time: 66.2 us; the launch traced here: 66 us
  Pallas kernels  61.5 us (93%)
  local copies, waits for them, and re-layouts  3.8 us (6%)
    pallas_call x1, Pallas kernels, shards(): pl.pallas_call(kernel, out_shape=[jax.ShapeDtypeStruct((NS, RL, COLS), BF...  61.5 us
    unnamed x7, local copies, waits for them, and re-layouts  3.8 us

profile of v1, /device:TPU:6, one launch (start us, length us, event | category | flops | bytes accessed | tf_op | source)
XLA Modules:
  0.0 66.0 jit_solution(18353359579636650220)
XLA Ops:
  0.6 61.5 %shard_map.85 = (bf16[8,128,512]{2,1,0:T(8,128)(2,1)}, bf16[8,128,128]{2,1,0:T(8,128)(2,1)}, bf16[256,128]{1,0:T(8,128)(2,1)}) custom-call(s32[8]{0:T(128)} %sp_ref.1, s32[8]{0:T(128)} %len_ref.1, bf16[8,128,512]{2,1,0:T(8,128)(2,1)} %bitcast.5, bf16[8,128,512]{2,1,0:T(8,128)(2,1)} %bitcast.6, bf16[8,128,128]{2,1,0:T(8,128)(2,1)} %bitcast.8, ...), custom_call_target="tpu_custom_call" | custom-call | tf_op jit(solution)/shard_map/pallas_call | solution.py:259
  62.2 0.0 copy-start
  62.2 2.3 %copy.12 = bf16[1024,512]{1,0:T(8,128)(2,1)} copy(bf16[1024,512]{1,0:T(8,128)(2,1)} %bitcast.7) | data formatting | bytes 2097152
  64.5 0.0 copy-done
  64.5 0.0 copy-start.1
  64.5 0.7 %copy.13 = bf16[1024,128]{1,0:T(8,128)(2,1)} copy(bf16[1024,128]{1,0:T(8,128)(2,1)S(1)} %bitcast.9) | data formatting | bytes 524288
  65.2 0.2 copy-done.1
  65.4 0.6 copy.14
Async XLA Ops:
  62.2 2.3 %copy-start = (bf16[8,128,128]{2,1,0:T(8,128)(2,1)S(1)}, bf16[8,128,128]{2,1,0:T(8,128)(2,1)}, u32[]{:S(2)}) copy-start(bf16[8,128,128]{2,1,0:T(8,128)(2,1)} %get-tuple-element.7) | copy-start | bytes 786436
  64.5 0.9 %copy-start.1 = (bf16[256,128]{1,0:T(8,128)(2,1)S(1)}, bf16[256,128]{1,0:T(8,128)(2,1)}, u32[]{:S(2)}) copy-start(bf16[256,128]{1,0:T(8,128)(2,1)} %get-tuple-element.14) | copy-start | bytes 196612

commit v2 on v1

v2 whole, which is shorter than its diff:
```python
import functools

import jax
import jax.numpy as jnp
from jax import lax
from jax.experimental import pallas as pl
from jax.experimental.pallas import tpu as pltpu
from jax.sharding import PartitionSpec as P

HD = 128
RL = 128
PL = 512
NP = 8
NS = 8
NH = 4
HALF = PL // 2
COLS = NH * RL
SCALE = HD ** (-0.5)
EXP2 = SCALE * 1.4426950408889634
F32 = jnp.float32
BF16 = jnp.bfloat16
MESH = pl.DeviceIdType.MESH
SENDS = 80


def nt(a, b):
    return lax.dot_general(a, b, (((1,), (1,)), ((), ())), preferred_element_type=F32)


def nn(a, b):
    return lax.dot_general(a, b, (((1,), (0,)), ((), ())), preferred_element_type=F32)


def tn(a, b):
    return lax.dot_general(a, b, (((0,), (0,)), ((), ())), preferred_element_type=F32)


def forward_part(q, do, keys, vals, causal):
    scores = nt(keys, q)
    if causal:
        row = lax.broadcasted_iota(jnp.int32, scores.shape, 0)
        col = lax.broadcasted_iota(jnp.int32, scores.shape, 1) % RL
        scores = jnp.where(row <= col, scores, -1e30)
    top = jnp.max(scores, axis=0, keepdims=True)
    expo = jnp.exp2((scores - top) * EXP2)
    dprob = nt(vals, do)
    total = jnp.sum(expo, axis=0, keepdims=True)
    delta = jnp.sum(expo * dprob, axis=0, keepdims=True)
    return expo, dprob, top, total, delta


def kernel(sp_ref, len_ref, q_hbm, do_hbm, resp_hbm, pref_hbm,
           dq_v, dr_ref, dp_out,
           own_a, own_b, sib_a, sib_b, resp, q_v, do_v, e_ref, dp_ref, ds_ref, st_ref, run, own_sum,
           rg, rg_send, rg_recv, sib_send, sib_recv, g_ref, y_recv, z_send, z_recv, prev_ref, last_ref,
           load_sem, send_sem, near_sem, far_sem, sib_sem, back_sem, y_sem, z_sem, resp_sem, rg_sem):
    group, tensor = lax.axis_index("group"), lax.axis_index("tensor")
    zh, y, c, kv = group // 8, (group // 2) % 4, group % 2, tensor % 2
    pair = tensor + 1 - 2 * kv
    owns, sibs = (own_a, own_b), (sib_a, sib_b)

    def device(dz, dy, dc, dl):
        g = ((zh + dz) % 2) * 8 + ((y + dy) % 4) * 2 + (c + dc) % 2
        return (g, pair if dl else tensor)

    sibling, across, high, far = (0, 0, 1, 0), (0, 0, 0, 1), (1, 0, 0, 0), (1, 0, 0, 1)
    ring = ((0, 1, 0, 0), (0, 3, 0, 0), (0, 2, 0, 0))
    peers = (sibling, across, high, far) + ring
    flying = []

    def send(src, dst, recv_sem, to):
        copy = pltpu.make_async_remote_copy(
            src, dst, send_sem.at[len(flying)], recv_sem, device_id=device(*to), device_id_type=MESH
        )
        copy.start()
        flying.append(copy)

    def arrived(ref, recv_sem):
        pltpu.make_async_remote_copy(
            ref, ref, send_sem.at[0], recv_sem, device_id=device(*sibling), device_id_type=MESH
        ).wait_recv()

    mine, there = zh * 4 + y, (1 - zh) * 4 + y
    loads = [pltpu.make_async_copy(pref_hbm.at[pl.ds(i * RL, RL)], owns[i].at[kv, mine], load_sem.at[8 + i]) for i in range(2)]
    loads.append(pltpu.make_async_copy(resp_hbm, resp.at[kv], load_sem.at[10]))
    for i, (src, dst) in enumerate(((q_hbm, q_v), (do_hbm, do_v))):
        for h in range(NH):
            loads.append(
                pltpu.make_async_copy(
                    src.at[:, :, pl.ds(h * HD, HD)], dst.at[:, pl.ds(h * RL, RL), :], load_sem.at[i * NH + h]
                )
            )
    for copy in loads:
        copy.start()
    barrier = pltpu.get_barrier_semaphore()
    for to in peers:
        pl.semaphore_signal(barrier, inc=1, device_id=device(*to), device_id_type=MESH)
    pl.semaphore_wait(barrier, len(peers))

    def near(i, k, p, to):
        unit = owns[i].at[k, p]
        send(unit, unit, near_sem.at[i, k, p], to)

    def wait_near(i, k, p):
        arrived(owns[i].at[k, p], near_sem.at[i, k, p])

    def mirror(i, src, dst, slot):
        send(src, dst, sib_sem.at[i, slot], sibling)

    for i in range(2):
        loads[i].wait()
        for to in (high, far, across):
            near(i, kv, mine, to)
    for i in range(2):
        for to in ring:
            near(i, kv, mine, to)
        mirror(i, owns[i].at[kv, mine], sibs[i].at[kv, mine], 0)
    for i in range(2):
        wait_near(i, 1 - kv, mine)
        for to in ring:
            near(i, 1 - kv, mine, to)
        mirror(i, owns[i].at[1 - kv, mine], sibs[i].at[1 - kv, mine], 1)
    for i in range(2):
        for k in (1 - kv, kv):
            wait_near(i, k, there)
        block = owns[i].at[:, there]
        for to in ring:
            send(block, block, far_sem.at[i, y], to)
        mirror(i, block, sibs[i].at[:, there], 2)
    loads[2].wait()
    send(resp.at[kv], resp.at[kv], resp_sem.at[0], across)

    for s in range(NS):
        at = jnp.int32(-1)
        for j in range(s):
            at = jnp.where(sp_ref[j] == sp_ref[s], j, at)
        prev_ref[s] = at
    for p in range(NP):
        at = jnp.int32(-1)
        for j in range(NS):
            at = jnp.where(sp_ref[j] == p, j, at)
        last_ref[p] = at
    for copy in loads[3:]:
        copy.wait()

    @pl.loop(0, NS)
    def _(s):
        row = lax.broadcasted_iota(jnp.int32, (COLS, HD), 0) % RL
        do_v[s] = jnp.where(row < len_ref[s], do_v[s], jnp.zeros((COLS, HD), BF16))

    def share(i):
        for j in range(3):
            dy = ring[j][1]
            at = (y - dy + 4) % 4
            p, q = zh * 4 + at, (1 - zh) * 4 + at
            wait_near(i, kv, p)
            wait_near(i, 1 - kv, p)
            mirror(i, owns[i].at[:, p], sibs[i].at[:, p], 3 + j)
        for j in range(3):
            dy = ring[j][1]
            at = (y - dy + 4) % 4
            q = (1 - zh) * 4 + at
            arrived(owns[i].at[:, q], far_sem.at[i, at])
            mirror(i, owns[i].at[:, q], sibs[i].at[:, q], 6 + j)

    def shared(i):
        arrived(sibs[i].at[kv, mine], sib_sem.at[i, 0])
        arrived(sibs[i].at[1 - kv, mine], sib_sem.at[i, 1])
        arrived(sibs[i].at[:, there], sib_sem.at[i, 2])
        for j in range(3):
            at = (y - ring[j][1] + 4) % 4
            arrived(sibs[i].at[:, zh * 4 + at], sib_sem.at[i, 3 + j])
            arrived(sibs[i].at[:, (1 - zh) * 4 + at], sib_sem.at[i, 6 + j])

    def block_of(k, part, s):
        if part == 2:
            return resp[k, s]
        p = sp_ref[s]
        return jnp.concatenate([owns[part][k, p], sibs[part][k, p]], axis=0)

    def forward(part):
        n = RL if part == 2 else HALF

        @pl.loop(0, NS, unroll=4)
        def _(s):
            expo, dprob, top, total, delta = forward_part(
                q_v[s], do_v[s], block_of(0, part, s), block_of(1, part, s), part == 2
            )
            e_ref[s, pl.ds(part * HALF, n)] = expo
            dp_ref[s, pl.ds(part * HALF, n)] = dprob
            st_ref[s, pl.ds(part, 1)] = top
            st_ref[s, pl.ds(3 + part, 1)] = total
            st_ref[s, pl.ds(6 + part, 1)] = delta

    arrived(resp.at[1 - kv], resp_sem.at[0])
    forward(2)
    share(0)
    shared(0)
    forward(0)
    share(1)
    shared(1)
    forward(1)

    @pl.loop(0, NS)
    def _(s):
        tops = st_ref[s, pl.ds(0, 3)]
        factor = jnp.exp2((tops - jnp.max(tops, axis=0, keepdims=True)) * EXP2)
        factor = factor / jnp.sum(factor * st_ref[s, pl.ds(3, 3)], axis=0, keepdims=True)
        st_ref[s, pl.ds(0, 3)] = factor
        st_ref[s, pl.ds(3, 1)] = jnp.sum(factor * st_ref[s, pl.ds(6, 3)], axis=0, keepdims=True)

    def backward(s, part):
        rows = pl.ds(part * HALF, RL if part == 2 else HALF)
        prob = e_ref[s, rows] * st_ref[s, pl.ds(part, 1)]
        ds = (prob * (dp_ref[s, rows] - st_ref[s, pl.ds(3, 1)])).astype(BF16)
        ds_ref[s, rows] = ds
        return nn(ds, q_v[s]) * SCALE, nn(prob.astype(BF16), do_v[s])

    def prefix_grads(i):
        @pl.loop(0, NS, unroll=4)
        def _(s):
            prev = prev_ref[s]
            at = jnp.maximum(prev, 0)
            for k, grad in enumerate(backward(s, i)):
                run[k, s] = grad + jnp.where(prev >= 0, run[k, at], 0.0)

        @pl.loop(0, NP)
        def _(p):
            last = last_ref[p]
            at = jnp.maximum(last, 0)
            for k in range(2):
                total = jnp.where(last >= 0, run[k, at], 0.0)
                own_sum[k, p] = total[:RL]
                sib_send[i, k, p] = total[RL:].astype(BF16)
        send(sib_send.at[i], sib_recv.at[i], back_sem.at[i], sibling)

    def reduce_ring(i):
        arrived(sib_recv.at[i], back_sem.at[i])

        @pl.loop(0, NP)
        def _(p):
            for k in range(2):
                g_ref[i, k, p // 4, p % 4] = (own_sum[k, p] + sib_recv[i, k, p].astype(F32)).astype(BF16)
        for j, to in enumerate(ring):
            send(g_ref.at[i, :, :, (y + to[1]) % 4], y_recv.at[i, j], y_sem.at[i, j], to)

    def reduce_high(i):
        for j in range(3):
            arrived(y_recv.at[i, j], y_sem.at[i, j])
        for j, to in enumerate((high, far, across)):
            z_send[i, j] = chip_total(i, (kv + to[3]) % 2, (zh + to[0]) % 2).astype(BF16)
            send(z_send.at[i, j], z_recv.at[i, j], z_sem.at[i, j], to)

    def chip_total(i, k, z):
        total = g_ref[i, k, z, y].astype(F32)
        for j in range(3):
            total = total + y_recv[i, j, k, z].astype(F32)
        return total

    def query_grads(first, count):
        @pl.loop(first, first + count, unroll=4)
        def _(s):
            p = sp_ref[s]
            keys = jnp.concatenate([block_of(0, part, s) for part in range(3)], axis=0)
            dqt = tn(keys, ds_ref[s]) * SCALE
            for h in range(NH):
                dq_v[s, :, pl.ds(h * HD, HD)] = dqt[:, h * RL:(h + 1) * RL].T.astype(BF16)

    prefix_grads(0)

    @pl.loop(0, NS, unroll=4)
    def _(s):
        for k, grad in enumerate(backward(s, 2)):
            rg[k, s] = grad
            rg_send[k, s] = grad.astype(BF16)

    send(rg_send.at[1 - kv], rg_recv, rg_sem.at[0], across)
    reduce_ring(0)
    prefix_grads(1)
    query_grads(0, 4)
    reduce_ring(1)
    query_grads(4, 4)
    arrived(rg_recv, rg_sem.at[0])

    @pl.loop(0, NS)
    def _(s):
        dr_ref[s] = (rg[kv, s] + rg_recv[s].astype(F32)).astype(BF16)

    for i in range(2):
        reduce_high(i)
    for i in range(2):
        total = chip_total(i, kv, zh)
        for j in (2, 1, 0):
            arrived(z_recv.at[i, j], z_sem.at[i, j])
            total = total + z_recv[i, j].astype(F32)
        dp_out[pl.ds(i * RL, RL)] = total.astype(BF16)
    for copy in flying:
        copy.wait_send()


def finish(*refs):
    sem = refs[-1]
    pairs = list(zip(refs[:3], refs[3:6]))
    copies = [pltpu.make_async_copy(src, dst, sem.at[i]) for i, (src, dst) in enumerate(pairs)]
    for copy in copies:
        copy.start()
    for copy in copies:
        copy.wait()


def shards(queries, resp_kv, prefix_kv, grad_out, lengths, slot_prompt):
    smem = pl.BlockSpec(memory_space=pltpu.SMEM)
    vmem = pl.BlockSpec(memory_space=pltpu.VMEM)
    hbm = pl.BlockSpec(memory_space=pltpu.HBM)
    dma = pltpu.SemaphoreType.DMA
    dq, dr, dp = pl.pallas_call(
        kernel,
        out_shape=[
            pltpu.VMEM((NS, RL, COLS), BF16),
            pltpu.VMEM((NS, RL, HD), BF16),
            pltpu.VMEM((HALF, HD), BF16),
        ],
        in_specs=[smem, smem, hbm, hbm, hbm, hbm],
        out_specs=[vmem, vmem, vmem],
        scratch_shapes=[
            pltpu.VMEM((2, NP, RL, HD), BF16),
            pltpu.VMEM((2, NP, RL, HD), BF16),
            pltpu.VMEM((2, NP, RL, HD), BF16),
            pltpu.VMEM((2, NP, RL, HD), BF16),
            pltpu.VMEM((2, NS, RL, HD), BF16),
            pltpu.VMEM((NS, COLS, HD), BF16),
            pltpu.VMEM((NS, COLS, HD), BF16),
            pltpu.VMEM((NS, PL + RL, COLS), F32),
            pltpu.VMEM((NS, PL + RL, COLS), F32),
            pltpu.VMEM((NS, PL + RL, COLS), BF16),
            pltpu.VMEM((NS, 16, COLS), F32),
            pltpu.VMEM((2, NS, HALF, HD), F32),
            pltpu.VMEM((2, NP, RL, HD), F32),
            pltpu.VMEM((2, NS, RL, HD), F32),
            pltpu.VMEM((2, NS, RL, HD), BF16),
            pltpu.VMEM((NS, RL, HD), BF16),
            pltpu.VMEM((2, 2, NP, RL, HD), BF16),
            pltpu.VMEM((2, 2, NP, RL, HD), BF16),
            pltpu.VMEM((2, 2, 2, 4, RL, HD), BF16),
            pltpu.VMEM((2, 3, 2, 2, RL, HD), BF16),
            pltpu.VMEM((2, 3, RL, HD), BF16),
            pltpu.VMEM((2, 3, RL, HD), BF16),
            pltpu.SMEM((NS,), jnp.int32),
            pltpu.SMEM((NP,), jnp.int32),
            dma((11,)),
            dma((SENDS,)),
            dma((2, 2, NP)),
            dma((2, 4)),
            dma((2, 9)),
            dma((2,)),
            dma((2, 3)),
            dma((2, 3)),
            dma((1,)),
            dma((1,)),
        ],
        compiler_params=pltpu.CompilerParams(
            collective_id=0, has_side_effects=True, vmem_limit_bytes=62 * 2**20
        ),
    )(
        slot_prompt,
        lengths,
        queries.reshape(NS, RL, COLS),
        grad_out.reshape(NS, RL, COLS),
        resp_kv.reshape(NS, RL, HD),
        prefix_kv,
    )
    return dq.reshape(NS * RL, COLS), dr.reshape(NS * RL, HD), dp


def solution(mesh):
    spec = P("group", "tensor")
    return jax.shard_map(
        shards,
        mesh=mesh,
        in_specs=(spec, spec, spec, spec, P("group"), P("group")),
        out_specs=(spec, spec, spec),
        check_vma=False,
    )
```

time: 66.2 us -> 60 us (0.906); the launches traced: 66 us -> 59.1 us
  Pallas kernels: 61.5 us -> 56.2 us
  local copies, waits for them, and re-layouts: 3.8 us -> 2.3 us
    pallas_call x1, Pallas kernels: 61.5 us -> 56.2 us  [shards(): pl.pallas_call(kernel, out_shape=[pltpu.VMEM((NS, RL, COLS), BF16), pltpu...]
    unnamed x7 -> x3, local copies, waits for them, and re-layouts: 3.8 us -> 2.3 us
where the time goes in v2:
time: 60 us; the launch traced here: 59.1 us
  Pallas kernels  56.2 us (94%)
  local copies, waits for them, and re-layouts  2.3 us (4%)
  between operations  0.64 us (1%)
    pallas_call x1, Pallas kernels, shards(): pl.pallas_call(kernel, out_shape=[pltpu.VMEM((NS, RL, COLS), BF16), pltpu...  56.2 us
    unnamed x3, local copies, waits for them, and re-layouts  2.3 us

profile of v2, /device:TPU:6, one launch (start us, length us, event | category | flops | bytes accessed | tf_op | source)
XLA Modules:
  0.0 59.1 jit_solution(8182859395388198939)
XLA Ops:
  0.6 56.2 %shard_map.85 = (bf16[8,128,512]{2,1,0:T(8,128)(2,1)S(1)}, bf16[8,128,128]{2,1,0:T(8,128)(2,1)S(1)}, bf16[256,128]{1,0:T(8,128)(2,1)S(1)}) custom-call(s32[8]{0:T(128)} %sp_ref.1, s32[8]{0:T(128)} %len_ref.1, bf16[8,128,512]{2,1,0:T(8,128)(2,1)} %bitcast.7, bf16[8,128,512]{2,1,0:T(8,128)(2,1)} %bitcast.8, bf16[8,128,128]{2,1,0:T(8,128)(2,1)} %bitcast.9, ...), custom_call_target="tpu_custom_call" | custom-call | tf_op jit(solution)/shard_map/pallas_call | solution.py:316
  56.8 1.0 %copy.12 = bf16[1024,512]{1,0:T(8,128)(2,1)} copy(bf16[1024,512]{1,0:T(8,128)(2,1)S(1)} %bitcast.5) | data formatting | bytes 2097152
  57.8 0.7 %copy.13 = bf16[1024,128]{1,0:T(8,128)(2,1)} copy(bf16[1024,128]{1,0:T(8,128)(2,1)S(1)} %bitcast.6) | data formatting | bytes 524288
  58.5 0.6 %copy.14 = bf16[256,128]{1,0:T(8,128)(2,1)} copy(bf16[256,128]{1,0:T(8,128)(2,1)S(1)} %get-tuple-element.11) | data formatting | bytes 131072

commit v3 on v2

v3 whole, which is shorter than its diff:
```python
import functools

import jax
import jax.numpy as jnp
from jax import lax
from jax.experimental import pallas as pl
from jax.experimental.pallas import tpu as pltpu
from jax.sharding import PartitionSpec as P

HD = 128
RL = 128
PL = 512
NP = 8
NS = 8
NH = 4
HALF = PL // 2
PARTS = 2
ROWS = HALF // PARTS
WIDE = 2 * ROWS
COLS = NH * RL
SCALE = HD ** (-0.5)
EXP2 = SCALE * 1.4426950408889634
F32 = jnp.float32
BF16 = jnp.bfloat16
MESH = pl.DeviceIdType.MESH
SENDS = 128


def nt(a, b):
    return lax.dot_general(a, b, (((1,), (1,)), ((), ())), preferred_element_type=F32)


def nn(a, b):
    return lax.dot_general(a, b, (((1,), (0,)), ((), ())), preferred_element_type=F32)


def tn(a, b):
    return lax.dot_general(a, b, (((0,), (0,)), ((), ())), preferred_element_type=F32)


def forward_part(q, do, keys, vals, causal):
    scores = nt(keys, q)
    if causal:
        row = lax.broadcasted_iota(jnp.int32, scores.shape, 0)
        col = lax.broadcasted_iota(jnp.int32, scores.shape, 1) % RL
        scores = jnp.where(row <= col, scores, -1e30)
    top = jnp.max(scores, axis=0, keepdims=True)
    expo = jnp.exp2((scores - top) * EXP2)
    dprob = nt(vals, do)
    total = jnp.sum(expo, axis=0, keepdims=True)
    delta = jnp.sum(expo * dprob, axis=0, keepdims=True)
    return expo, dprob, top, total, delta


def kernel(sp_ref, len_ref, q_hbm, do_hbm, resp_hbm, pref_hbm,
           dq_v, dr_ref, dp_out,
           *scratch):
    owns, sibs = scratch[:PARTS], scratch[PARTS:2 * PARTS]
    (resp, q_v, do_v, e_ref, dp_ref, ds_ref, st_ref, run, own_sum,
     rg, rg_send, rg_recv, sib_send, sib_recv, g_ref, y_recv, z_send, z_recv, prev_ref, last_ref,
     load_sem, send_sem, near_sem, far_sem, sib_sem, back_sem, y_sem, z_sem, resp_sem, rg_sem) = scratch[2 * PARTS:]
    group, tensor = lax.axis_index("group"), lax.axis_index("tensor")
    zh, y, c, kv = group // 8, (group // 2) % 4, group % 2, tensor % 2
    pair = tensor + 1 - 2 * kv

    def device(dz, dy, dc, dl):
        g = ((zh + dz) % 2) * 8 + ((y + dy) % 4) * 2 + (c + dc) % 2
        return (g, pair if dl else tensor)

    sibling, across, high, far = (0, 0, 1, 0), (0, 0, 0, 1), (1, 0, 0, 0), (1, 0, 0, 1)
    ring = ((0, 1, 0, 0), (0, 3, 0, 0), (0, 2, 0, 0))
    peers = (sibling, across, high, far) + ring
    flying = []

    def send(src, dst, recv_sem, to):
        copy = pltpu.make_async_remote_copy(
            src, dst, send_sem.at[len(flying)], recv_sem, device_id=device(*to), device_id_type=MESH
        )
        copy.start()
        flying.append(copy)

    def arrived(ref, recv_sem):
        pltpu.make_async_remote_copy(
            ref, ref, send_sem.at[0], recv_sem, device_id=device(*sibling), device_id_type=MESH
        ).wait_recv()

    mine, there = zh * 4 + y, (1 - zh) * 4 + y
    loads = [pltpu.make_async_copy(pref_hbm.at[pl.ds(i * ROWS, ROWS)], owns[i].at[kv, mine], load_sem.at[9 + i]) for i in range(PARTS)]
    loads.append(pltpu.make_async_copy(resp_hbm, resp.at[kv], load_sem.at[8]))
    for i, (src, dst) in enumerate(((q_hbm, q_v), (do_hbm, do_v))):
        for h in range(NH):
            loads.append(
                pltpu.make_async_copy(
                    src.at[:, :, pl.ds(h * HD, HD)], dst.at[:, pl.ds(h * RL, RL), :], load_sem.at[i * NH + h]
                )
            )
    for copy in loads:
        copy.start()
    barrier = pltpu.get_barrier_semaphore()
    for to in peers:
        pl.semaphore_signal(barrier, inc=1, device_id=device(*to), device_id_type=MESH)
    pl.semaphore_wait(barrier, len(peers))

    def near(i, k, p, to):
        unit = owns[i].at[k, p]
        send(unit, unit, near_sem.at[i, k, p], to)

    def wait_near(i, k, p):
        arrived(owns[i].at[k, p], near_sem.at[i, k, p])

    def mirror(i, src, dst, slot):
        send(src, dst, sib_sem.at[i, slot], sibling)

    for i in range(PARTS):
        loads[i].wait()
        for to in (across, far, high):
            near(i, kv, mine, to)
    for i in range(PARTS):
        for to in ring:
            near(i, kv, mine, to)
    for i in range(PARTS):
        wait_near(i, 1 - kv, mine)
        for to in ring:
            near(i, 1 - kv, mine, to)
    for i in range(PARTS):
        for k in (1 - kv, kv):
            wait_near(i, k, there)
        block = owns[i].at[:, there]
        for to in ring:
            send(block, block, far_sem.at[i, y], to)
    loads[PARTS].wait()
    send(resp.at[kv], resp.at[kv], resp_sem.at[0], across)

    for s in range(NS):
        at = jnp.int32(-1)
        for j in range(s):
            at = jnp.where(sp_ref[j] == sp_ref[s], j, at)
        prev_ref[s] = at
    for p in range(NP):
        at = jnp.int32(-1)
        for j in range(NS):
            at = jnp.where(sp_ref[j] == p, j, at)
        last_ref[p] = at
    for copy in loads[PARTS + 1:]:
        copy.wait()

    @pl.loop(0, NS)
    def _(s):
        row = lax.broadcasted_iota(jnp.int32, (COLS, HD), 0) % RL
        do_v[s] = jnp.where(row < len_ref[s], do_v[s], jnp.zeros((COLS, HD), BF16))

    def share(i):
        for j in range(3):
            p = zh * 4 + (y - ring[j][1] + 4) % 4
            wait_near(i, kv, p)
            wait_near(i, 1 - kv, p)
        block = pl.ds(zh * 4, 4)
        mirror(i, owns[i].at[:, block], sibs[i].at[:, block], 0)
        for j in range(3):
            at = (y - ring[j][1] + 4) % 4
            arrived(owns[i].at[:, (1 - zh) * 4 + at], far_sem.at[i, at])
        block = pl.ds(4 - zh * 4, 4)
        mirror(i, owns[i].at[:, block], sibs[i].at[:, block], 1)

    def shared(i):
        for j, first in enumerate((zh * 4, 4 - zh * 4)):
            arrived(sibs[i].at[:, pl.ds(first, 4)], sib_sem.at[i, j])

    def block_of(k, part, s):
        if part == PARTS:
            return resp[k, s]
        p = sp_ref[s]
        return jnp.concatenate([owns[part][k, p], sibs[part][k, p]], axis=0)

    def forward(part):
        n = RL if part == PARTS else WIDE

        @pl.loop(0, NS, unroll=8)
        def _(s):
            expo, dprob, top, total, delta = forward_part(
                q_v[s], do_v[s], block_of(0, part, s), block_of(1, part, s), part == PARTS
            )
            e_ref[s, pl.ds(part * WIDE, n)] = expo
            dp_ref[s, pl.ds(part * WIDE, n)] = dprob
            st_ref[s, pl.ds(part, 1)] = top
            st_ref[s, pl.ds(PARTS + 1 + part, 1)] = total
            st_ref[s, pl.ds(2 * PARTS + 2 + part, 1)] = delta

    share(0)
    shared(0)
    forward(0)
    share(1)
    arrived(resp.at[1 - kv], resp_sem.at[0])
    forward(PARTS)
    shared(1)
    forward(1)

    @pl.loop(0, NS)
    def _(s):
        tops = st_ref[s, pl.ds(0, PARTS + 1)]
        factor = jnp.exp2((tops - jnp.max(tops, axis=0, keepdims=True)) * EXP2)
        factor = factor / jnp.sum(factor * st_ref[s, pl.ds(PARTS + 1, PARTS + 1)], axis=0, keepdims=True)
        st_ref[s, pl.ds(0, PARTS + 1)] = factor
        st_ref[s, pl.ds(PARTS + 1, 1)] = jnp.sum(factor * st_ref[s, pl.ds(2 * PARTS + 2, PARTS + 1)], axis=0, keepdims=True)

    def backward(s, part):
        rows = pl.ds(part * WIDE, RL if part == PARTS else WIDE)
        prob = e_ref[s, rows] * st_ref[s, pl.ds(part, 1)]
        ds = (prob * (dp_ref[s, rows] - st_ref[s, pl.ds(PARTS + 1, 1)])).astype(BF16)
        ds_ref[s, rows] = ds
        return nn(ds, q_v[s]) * SCALE, nn(prob.astype(BF16), do_v[s])

    def prefix_grads(i, middle=None):
        def slot_grads(s):
            prev = prev_ref[s]
            at = jnp.maximum(prev, 0)
            for k, grad in enumerate(backward(s, i)):
                run[k, s] = grad + jnp.where(prev >= 0, run[k, at], 0.0)

        pl.loop(0, NS // 2, unroll=4)(slot_grads)
        if middle is not None:
            reduce_ring(middle)
        pl.loop(NS // 2, NS, unroll=4)(slot_grads)

        @pl.loop(0, NP)
        def _(p):
            last = last_ref[p]
            at = jnp.maximum(last, 0)
            for k in range(2):
                total = jnp.where(last >= 0, run[k, at], 0.0)
                own_sum[i, k, p] = total[:ROWS]
                sib_send[i, k, p] = total[ROWS:].astype(BF16)
        send(sib_send.at[i], sib_recv.at[i], back_sem.at[i], sibling)

    def reduce_ring(i):
        arrived(sib_recv.at[i], back_sem.at[i])
        for side in range(2):
            z = (zh + 1 - side) % 2

            @pl.loop(0, 4)
            def _(p):
                for k in range(2):
                    both = own_sum[i, k, z * 4 + p] + sib_recv[i, k, z * 4 + p].astype(F32)
                    g_ref[i, side, p, k] = both.astype(BF16)
            for j, to in enumerate(ring):
                send(g_ref.at[i, side, (y + to[1]) % 4], y_recv.at[i, side, j], y_sem.at[i, side, j], to)

    def chip_total(i, side, k):
        total = g_ref[i, side, y, k].astype(F32)
        for j in range(3):
            total = total + y_recv[i, side, j, k].astype(F32)
        return total

    def reduce_high(i, side):
        for j in range(3):
            arrived(y_recv.at[i, side, j], y_sem.at[i, side, j])
        for j, to in enumerate((high, far, across)):
            if to[0] != side:
                z_send[i, j] = chip_total(i, side, (kv + to[3]) % 2).astype(BF16)
                send(z_send.at[i, j], z_recv.at[i, j], z_sem.at[i, j], to)

    def query_grads(first, count):
        @pl.loop(first, first + count, unroll=4)
        def _(s):
            p = sp_ref[s]
            keys = jnp.concatenate([block_of(0, part, s) for part in range(PARTS + 1)], axis=0)
            dqt = tn(keys, ds_ref[s]) * SCALE
            for h in range(NH):
                dq_v[s, :, pl.ds(h * HD, HD)] = dqt[:, h * RL:(h + 1) * RL].T.astype(BF16)

    prefix_grads(0)

    @pl.loop(0, NS, unroll=4)
    def _(s):
        for k, grad in enumerate(backward(s, PARTS)):
            rg[k, s] = grad
            rg_send[k, s] = grad.astype(BF16)

    send(rg_send.at[1 - kv], rg_recv, rg_sem.at[0], across)
    for i in range(1, PARTS):
        prefix_grads(i, i - 1)
    query_grads(0, 4)
    reduce_ring(PARTS - 1)
    query_grads(4, 4)
    arrived(rg_recv, rg_sem.at[0])

    @pl.loop(0, NS)
    def _(s):
        dr_ref[s] = (rg[kv, s] + rg_recv[s].astype(F32)).astype(BF16)

    for i in range(PARTS):
        for side in range(2):
            reduce_high(i, side)
    for i in range(PARTS):
        total = chip_total(i, 1, kv)
        for j in (2, 1, 0):
            arrived(z_recv.at[i, j], z_sem.at[i, j])
            total = total + z_recv[i, j].astype(F32)
        dp_out[pl.ds(i * ROWS, ROWS)] = total.astype(BF16)
    for copy in flying:
        copy.wait_send()


def finish(*refs):
    sem = refs[-1]
    pairs = list(zip(refs[:3], refs[3:6]))
    copies = [pltpu.make_async_copy(src, dst, sem.at[i]) for i, (src, dst) in enumerate(pairs)]
    for copy in copies:
        copy.start()
    for copy in copies:
        copy.wait()


def shards(queries, resp_kv, prefix_kv, grad_out, lengths, slot_prompt):
    smem = pl.BlockSpec(memory_space=pltpu.SMEM)
    vmem = pl.BlockSpec(memory_space=pltpu.VMEM)
    hbm = pl.BlockSpec(memory_space=pltpu.HBM)
    dma = pltpu.SemaphoreType.DMA
    dq, dr, dp = pl.pallas_call(
        kernel,
        out_shape=[
            pltpu.VMEM((NS, RL, COLS), BF16),
            pltpu.VMEM((NS, RL, HD), BF16),
            pltpu.VMEM((HALF, HD), BF16),
        ],
        in_specs=[smem, smem, hbm, hbm, hbm, hbm],
        out_specs=[vmem, vmem, vmem],
        scratch_shapes=[pltpu.VMEM((2, NP, ROWS, HD), BF16)] * (2 * PARTS) + [
            pltpu.VMEM((2, NS, RL, HD), BF16),
            pltpu.VMEM((NS, COLS, HD), BF16),
            pltpu.VMEM((NS, COLS, HD), BF16),
            pltpu.VMEM((NS, PL + RL, COLS), F32),
            pltpu.VMEM((NS, PL + RL, COLS), F32),
            pltpu.VMEM((NS, PL + RL, COLS), BF16),
            pltpu.VMEM((NS, 16, COLS), F32),
            pltpu.VMEM((2, NS, WIDE, HD), F32),
            pltpu.VMEM((PARTS, 2, NP, ROWS, HD), F32),
            pltpu.VMEM((2, NS, RL, HD), F32),
            pltpu.VMEM((2, NS, RL, HD), BF16),
            pltpu.VMEM((NS, RL, HD), BF16),
            pltpu.VMEM((PARTS, 2, NP, ROWS, HD), BF16),
            pltpu.VMEM((PARTS, 2, NP, ROWS, HD), BF16),
            pltpu.VMEM((PARTS, 2, 4, 2, ROWS, HD), BF16),
            pltpu.VMEM((PARTS, 2, 3, 2, ROWS, HD), BF16),
            pltpu.VMEM((PARTS, 3, ROWS, HD), BF16),
            pltpu.VMEM((PARTS, 3, ROWS, HD), BF16),
            pltpu.SMEM((NS,), jnp.int32),
            pltpu.SMEM((NP,), jnp.int32),
            dma((9 + PARTS,)),
            dma((SENDS,)),
            dma((PARTS, 2, NP)),
            dma((PARTS, 4)),
            dma((PARTS, 2)),
            dma((PARTS,)),
            dma((PARTS, 2, 3)),
            dma((PARTS, 3)),
            dma((1,)),
            dma((1,)),
        ],
        compiler_params=pltpu.CompilerParams(
            collective_id=0, has_side_effects=True, vmem_limit_bytes=62 * 2**20
        ),
    )(
        slot_prompt,
        lengths,
        queries.reshape(NS, RL, COLS),
        grad_out.reshape(NS, RL, COLS),
        resp_kv.reshape(NS, RL, HD),
        prefix_kv,
    )
    return dq.reshape(NS * RL, COLS), dr.reshape(NS * RL, HD), dp


def solution(mesh):
    spec = P("group", "tensor")
    return jax.shard_map(
        shards,
        mesh=mesh,
        in_specs=(spec, spec, spec, spec, P("group"), P("group")),
        out_specs=(spec, spec, spec),
        check_vma=False,
    )
```

time: 60 us -> 54.2 us (0.903); the launches traced: 59.1 us -> 54.1 us
  Pallas kernels: 56.2 us -> 51.2 us
    pallas_call x1, Pallas kernels: 56.2 us -> 51.2 us  [shards(): pl.pallas_call(kernel, out_shape=[pltpu.VMEM((NS, RL, COLS), BF16), pltpu...]
where the time goes in v3:
time: 54.2 us; the launch traced here: 54.1 us
  Pallas kernels  51.2 us (94%)
  local copies, waits for them, and re-layouts  2.3 us (4%)
  between operations  0.64 us (1%)
    pallas_call x1, Pallas kernels, shards(): pl.pallas_call(kernel, out_shape=[pltpu.VMEM((NS, RL, COLS), BF16), pltpu...  51.2 us
    unnamed x3, local copies, waits for them, and re-layouts  2.3 us

profile of v3, /device:TPU:6, one launch (start us, length us, event | category | flops | bytes accessed | tf_op | source)
XLA Modules:
  0.0 54.1 jit_solution(2671105676556890347)
XLA Ops:
  0.6 51.2 %shard_map.85 = (bf16[8,128,512]{2,1,0:T(8,128)(2,1)S(1)}, bf16[8,128,128]{2,1,0:T(8,128)(2,1)S(1)}, bf16[256,128]{1,0:T(8,128)(2,1)S(1)}) custom-call(s32[8]{0:T(128)} %sp_ref.1, s32[8]{0:T(128)} %len_ref.1, bf16[8,128,512]{2,1,0:T(8,128)(2,1)} %bitcast.7, bf16[8,128,512]{2,1,0:T(8,128)(2,1)} %bitcast.8, bf16[8,128,128]{2,1,0:T(8,128)(2,1)} %bitcast.9, ...), custom_call_target="tpu_custom_call" | custom-call | tf_op jit(solution)/shard_map/pallas_call | solution.py:319
  51.8 1.0 %copy.12 = bf16[1024,512]{1,0:T(8,128)(2,1)} copy(bf16[1024,512]{1,0:T(8,128)(2,1)S(1)} %bitcast.5) | data formatting | bytes 2097152
  52.8 0.7 %copy.13 = bf16[1024,128]{1,0:T(8,128)(2,1)} copy(bf16[1024,128]{1,0:T(8,128)(2,1)S(1)} %bitcast.6) | data formatting | bytes 524288
  53.5 0.6 %copy.14 = bf16[256,128]{1,0:T(8,128)(2,1)} copy(bf16[256,128]{1,0:T(8,128)(2,1)S(1)} %get-tuple-element.11) | data formatting | bytes 131072

commit v4 on v3

--- a/solution.py
+++ b/solution.py
@@ -23,7 +23,8 @@
 F32 = jnp.float32
 BF16 = jnp.bfloat16
 MESH = pl.DeviceIdType.MESH
-SENDS = 128
+SENDS = 64
+UNROLL = 8
 
 
 def nt(a, b):
@@ -52,12 +53,12 @@
     return expo, dprob, top, total, delta
 
 
-def kernel(sp_ref, len_ref, q_hbm, do_hbm, resp_hbm, pref_hbm,
+def kernel(sp_hbm, len_hbm, q_hbm, do_hbm, resp_hbm, pref_hbm,
            dq_v, dr_ref, dp_out,
            *scratch):
     owns, sibs = scratch[:PARTS], scratch[PARTS:2 * PARTS]
     (resp, q_v, do_v, e_ref, dp_ref, ds_ref, st_ref, run, own_sum,
-     rg, rg_send, rg_recv, sib_send, sib_recv, g_ref, y_recv, z_send, z_recv, prev_ref, last_ref,
+     rg, rg_send, rg_recv, sib_send, sib_recv, g_ref, y_recv, z_send, z_recv, sp_ref, len_ref, prev_ref, last_ref,
      load_sem, send_sem, near_sem, far_sem, sib_sem, back_sem, y_sem, z_sem, resp_sem, rg_sem) = scratch[2 * PARTS:]
     group, tensor = lax.axis_index("group"), lax.axis_index("tensor")
     zh, y, c, kv = group // 8, (group // 2) % 4, group % 2, tensor % 2
@@ -84,9 +85,14 @@
             ref, ref, send_sem.at[0], recv_sem, device_id=device(*sibling), device_id_type=MESH
         ).wait_recv()
 
+    barrier = pltpu.get_barrier_semaphore()
+    for to in peers:
+        pl.semaphore_signal(barrier, inc=1, device_id=device(*to), device_id_type=MESH)
     mine, there = zh * 4 + y, (1 - zh) * 4 + y
     loads = [pltpu.make_async_copy(pref_hbm.at[pl.ds(i * ROWS, ROWS)], owns[i].at[kv, mine], load_sem.at[9 + i]) for i in range(PARTS)]
     loads.append(pltpu.make_async_copy(resp_hbm, resp.at[kv], load_sem.at[8]))
+    for i, (src, dst) in enumerate(((sp_hbm, sp_ref), (len_hbm, len_ref))):
+        loads.append(pltpu.make_async_copy(src, dst, load_sem.at[9 + PARTS + i]))
     for i, (src, dst) in enumerate(((q_hbm, q_v), (do_hbm, do_v))):
         for h in range(NH):
             loads.append(
@@ -96,9 +102,6 @@
             )
     for copy in loads:
         copy.start()
-    barrier = pltpu.get_barrier_semaphore()
-    for to in peers:
-        pl.semaphore_signal(barrier, inc=1, device_id=device(*to), device_id_type=MESH)
     pl.semaphore_wait(barrier, len(peers))
 
     def near(i, k, p, to):
@@ -131,6 +134,8 @@
     loads[PARTS].wait()
     send(resp.at[kv], resp.at[kv], resp_sem.at[0], across)
 
+    for copy in loads[PARTS + 1:]:
+        copy.wait()
     for s in range(NS):
         at = jnp.int32(-1)
         for j in range(s):
@@ -141,8 +146,6 @@
         for j in range(NS):
             at = jnp.where(sp_ref[j] == p, j, at)
         last_ref[p] = at
-    for copy in loads[PARTS + 1:]:
-        copy.wait()
 
     @pl.loop(0, NS)
     def _(s):
@@ -203,34 +206,40 @@
         st_ref[s, pl.ds(0, PARTS + 1)] = factor
         st_ref[s, pl.ds(PARTS + 1, 1)] = jnp.sum(factor * st_ref[s, pl.ds(2 * PARTS + 2, PARTS + 1)], axis=0, keepdims=True)
 
-    def backward(s, part):
-        rows = pl.ds(part * WIDE, RL if part == PARTS else WIDE)
+    def backward(s, part, first, n):
+        rows = pl.ds(part * WIDE + first, n)
         prob = e_ref[s, rows] * st_ref[s, pl.ds(part, 1)]
         ds = (prob * (dp_ref[s, rows] - st_ref[s, pl.ds(PARTS + 1, 1)])).astype(BF16)
         ds_ref[s, rows] = ds
         return nn(ds, q_v[s]) * SCALE, nn(prob.astype(BF16), do_v[s])
 
-    def prefix_grads(i, middle=None):
-        def slot_grads(s):
+    def prefix_grads(i, first, save):
+        @pl.loop(0, NS, unroll=UNROLL)
+        def _(s):
             prev = prev_ref[s]
             at = jnp.maximum(prev, 0)
-            for k, grad in enumerate(backward(s, i)):
+            for k, grad in enumerate(backward(s, i, first, ROWS)):
                 run[k, s] = grad + jnp.where(prev >= 0, run[k, at], 0.0)
-
-        pl.loop(0, NS // 2, unroll=4)(slot_grads)
-        if middle is not None:
-            reduce_ring(middle)
-        pl.loop(NS // 2, NS, unroll=4)(slot_grads)
 
         @pl.loop(0, NP)
         def _(p):
             last = last_ref[p]
             at = jnp.maximum(last, 0)
             for k in range(2):
-                total = jnp.where(last >= 0, run[k, at], 0.0)
-                own_sum[i, k, p] = total[:ROWS]
-                sib_send[i, k, p] = total[ROWS:].astype(BF16)
+                save(k, p, jnp.where(last >= 0, run[k, at], 0.0))
+
+    def sibling_grads(i):
+        def save(k, p, total):
+            sib_send[i, k, p] = total.astype(BF16)
+
+        prefix_grads(i, ROWS, save)
         send(sib_send.at[i], sib_recv.at[i], back_sem.at[i], sibling)
+
+    def own_grads(i):
+        def save(k, p, total):
+            own_sum[i, k, p] = total
+
+        prefix_grads(i, 0, save)
 
     def reduce_ring(i):
         arrived(sib_recv.at[i], back_sem.at[i])
@@ -268,29 +277,32 @@
             for h in range(NH):
                 dq_v[s, :, pl.ds(h * HD, HD)] = dqt[:, h * RL:(h + 1) * RL].T.astype(BF16)
 
-    prefix_grads(0)
+    sibling_grads(0)
+    own_grads(0)
+    reduce_ring(0)
 
     @pl.loop(0, NS, unroll=4)
     def _(s):
-        for k, grad in enumerate(backward(s, PARTS)):
+        for k, grad in enumerate(backward(s, PARTS, 0, RL)):
             rg[k, s] = grad
             rg_send[k, s] = grad.astype(BF16)
 
     send(rg_send.at[1 - kv], rg_recv, rg_sem.at[0], across)
-    for i in range(1, PARTS):
-        prefix_grads(i, i - 1)
+    sibling_grads(1)
+    own_grads(1)
     query_grads(0, 4)
-    reduce_ring(PARTS - 1)
+    reduce_ring(1)
     query_grads(4, 4)
+    reduce_high(0, 0)
+    reduce_high(0, 1)
     arrived(rg_recv, rg_sem.at[0])
 
     @pl.loop(0, NS)
     def _(s):
         dr_ref[s] = (rg[kv, s] + rg_recv[s].astype(F32)).astype(BF16)
 
-    for i in range(PARTS):
-        for side in range(2):
-            reduce_high(i, side)
+    reduce_high(1, 0)
+    reduce_high(1, 1)
     for i in range(PARTS):
         total = chip_total(i, 1, kv)
         for j in (2, 1, 0):
@@ -312,7 +324,6 @@
 
 
 def shards(queries, resp_kv, prefix_kv, grad_out, lengths, slot_prompt):
-    smem = pl.BlockSpec(memory_space=pltpu.SMEM)
     vmem = pl.BlockSpec(memory_space=pltpu.VMEM)
     hbm = pl.BlockSpec(memory_space=pltpu.HBM)
     dma = pltpu.SemaphoreType.DMA
@@ -323,7 +334,7 @@
             pltpu.VMEM((NS, RL, HD), BF16),
             pltpu.VMEM((HALF, HD), BF16),
         ],
-        in_specs=[smem, smem, hbm, hbm, hbm, hbm],
+        in_specs=[hbm, hbm, hbm, hbm, hbm, hbm],
         out_specs=[vmem, vmem, vmem],
         scratch_shapes=[pltpu.VMEM((2, NP, ROWS, HD), BF16)] * (2 * PARTS) + [
             pltpu.VMEM((2, NS, RL, HD), BF16),
@@ -333,7 +344,7 @@
             pltpu.VMEM((NS, PL + RL, COLS), F32),
             pltpu.VMEM((NS, PL + RL, COLS), BF16),
             pltpu.VMEM((NS, 16, COLS), F32),
-            pltpu.VMEM((2, NS, WIDE, HD), F32),
+            pltpu.VMEM((2, NS, ROWS, HD), F32),
             pltpu.VMEM((PARTS, 2, NP, ROWS, HD), F32),
             pltpu.VMEM((2, NS, RL, HD), F32),
             pltpu.VMEM((2, NS, RL, HD), BF16),
@@ -345,8 +356,10 @@
             pltpu.VMEM((PARTS, 3, ROWS, HD), BF16),
             pltpu.VMEM((PARTS, 3, ROWS, HD), BF16),
             pltpu.SMEM((NS,), jnp.int32),
+            pltpu.SMEM((NS,), jnp.int32),
+            pltpu.SMEM((NS,), jnp.int32),
             pltpu.SMEM((NP,), jnp.int32),
-            dma((9 + PARTS,)),
+            dma((11 + PARTS,)),
             dma((SENDS,)),
             dma((PARTS, 2, NP)),
             dma((PARTS, 4)),

time: 54.2 us -> 52 us (0.959)
  Pallas kernels: 51.2 us -> 48.8 us
    pallas_call x1, Pallas kernels: 51.2 us -> 48.8 us  [shards(): pl.pallas_call(kernel, out_shape=[pltpu.VMEM((NS, RL, COLS), BF16), pltpu...]
where the time goes in v4:
time: 52 us; the launch traced here: 51.7 us
  Pallas kernels  48.8 us (94%)
  local copies, waits for them, and re-layouts  2.3 us (4%)
  between operations  0.64 us (1%)
    pallas_call x1, Pallas kernels, shards(): pl.pallas_call(kernel, out_shape=[pltpu.VMEM((NS, RL, COLS), BF16), pltpu...  48.8 us
    unnamed x3, local copies, waits for them, and re-layouts  2.3 us

profile of v4, /device:TPU:6, one launch (start us, length us, event | category | flops | bytes accessed | tf_op | source)
XLA Modules:
  0.0 51.7 jit_solution(2685959688121032398)
XLA Ops:
  0.6 48.8 %shard_map.85 = (bf16[8,128,512]{2,1,0:T(8,128)(2,1)S(1)}, bf16[8,128,128]{2,1,0:T(8,128)(2,1)S(1)}, bf16[256,128]{1,0:T(8,128)(2,1)S(1)}) custom-call(s32[8]{0:T(128)} %sp_hbm.1, s32[8]{0:T(128)} %len_hbm.1, bf16[8,128,512]{2,1,0:T(8,128)(2,1)} %bitcast.7, bf16[8,128,512]{2,1,0:T(8,128)(2,1)} %bitcast.8, bf16[8,128,128]{2,1,0:T(8,128)(2,1)} %bitcast.9, ...), custom_call_target="tpu_custom_call" | custom-call | tf_op jit(solution)/shard_map/pallas_call | solution.py:330
  49.4 1.0 %copy.12 = bf16[1024,512]{1,0:T(8,128)(2,1)} copy(bf16[1024,512]{1,0:T(8,128)(2,1)S(1)} %bitcast.5) | data formatting | bytes 2097152
  50.4 0.7 %copy.13 = bf16[1024,128]{1,0:T(8,128)(2,1)} copy(bf16[1024,128]{1,0:T(8,128)(2,1)S(1)} %bitcast.6) | data formatting | bytes 524288
  51.1 0.6 %copy.14 = bf16[256,128]{1,0:T(8,128)(2,1)} copy(bf16[256,128]{1,0:T(8,128)(2,1)S(1)} %get-tuple-element.11) | data formatting | bytes 131072

commit v5 on v4

--- a/solution.py
+++ b/solution.py
@@ -69,7 +69,7 @@
         return (g, pair if dl else tensor)
 
     sibling, across, high, far = (0, 0, 1, 0), (0, 0, 0, 1), (1, 0, 0, 0), (1, 0, 0, 1)
-    ring = ((0, 1, 0, 0), (0, 3, 0, 0), (0, 2, 0, 0))
+    ring = ((0, 2, 0, 0), (0, 1, 0, 0), (0, 3, 0, 0))
     peers = (sibling, across, high, far) + ring
     flying = []
 

time: 52 us -> 51.4 us (0.988)
  Pallas kernels: 48.8 us -> 48 us
    pallas_call x1, Pallas kernels: 48.8 us -> 48 us  [shards(): pl.pallas_call(kernel, out_shape=[pltpu.VMEM((NS, RL, COLS), BF16), pltpu...]
where the time goes in v5:
time: 51.4 us; the launch traced here: 51 us
  Pallas kernels  48 us (93%)
  local copies, waits for them, and re-layouts  2.3 us (4%)
  between operations  0.64 us (1%)
    pallas_call x1, Pallas kernels, shards(): pl.pallas_call(kernel, out_shape=[pltpu.VMEM((NS, RL, COLS), BF16), pltpu...  48 us
    unnamed x3, local copies, waits for them, and re-layouts  2.3 us

profile of v5, /device:TPU:6, one launch (start us, length us, event | category | flops | bytes accessed | tf_op | source)
XLA Modules:
  0.0 51.0 jit_solution(12809903002749505223)
XLA Ops:
  0.6 48.0 %shard_map.85 = (bf16[8,128,512]{2,1,0:T(8,128)(2,1)S(1)}, bf16[8,128,128]{2,1,0:T(8,128)(2,1)S(1)}, bf16[256,128]{1,0:T(8,128)(2,1)S(1)}) custom-call(s32[8]{0:T(128)} %sp_hbm.1, s32[8]{0:T(128)} %len_hbm.1, bf16[8,128,512]{2,1,0:T(8,128)(2,1)} %bitcast.7, bf16[8,128,512]{2,1,0:T(8,128)(2,1)} %bitcast.8, bf16[8,128,128]{2,1,0:T(8,128)(2,1)} %bitcast.9, ...), custom_call_target="tpu_custom_call" | custom-call | tf_op jit(solution)/shard_map/pallas_call | solution.py:330
  48.7 1.0 %copy.12 = bf16[1024,512]{1,0:T(8,128)(2,1)} copy(bf16[1024,512]{1,0:T(8,128)(2,1)S(1)} %bitcast.5) | data formatting | bytes 2097152
  49.6 0.7 %copy.13 = bf16[1024,128]{1,0:T(8,128)(2,1)} copy(bf16[1024,128]{1,0:T(8,128)(2,1)S(1)} %bitcast.6) | data formatting | bytes 524288
  50.3 0.6 %copy.14 = bf16[256,128]{1,0:T(8,128)(2,1)} copy(bf16[256,128]{1,0:T(8,128)(2,1)S(1)} %get-tuple-element.11) | data formatting | bytes 131072
